TPU v7x, 512 devices: a whole 4x4x16 slice. The times are simulated.
512 devices in a mesh: row: 32 (over x_hi, z), col: 16 (over y, x_lo, core).
Axes of the slice: x: 4 (x_hi: 2, x_lo: 2; x = x_hi * 2 + x_lo), y: 4, z: 16, core: 2. Of those that a mesh axis runs over, the one named last changes fastest.
Arguments:
- pair_elements: bfloat16 [1024, 61440], P(('row', 'col')), may hold values from -6 to 6
- energy_gaps: float32 [1024], replicated, may hold values from 0.5 to 3
- frequencies: float32 [3], replicated, may hold values from 0.3 to 3
Outputs:
- polarizability: bfloat16 [3, 4096, 61440], P(None, 'row', 'col')
All inputs are finite; a program needn't handle non-finite values.
Results may differ from a plain program's by a relative error of at most 0.0048.
Values may be sent and summed in bfloat16 or wider, within the bound.
A program may use at most 64 MiB of HBM per device.

v0:
```python
import functools
import math

import jax
import jax.numpy as jnp
from jax import lax
from jax.experimental import pallas as pl
from jax.experimental.pallas import tpu as pltpu
from jax.sharding import PartitionSpec as P

NW = 3
GSR = 128
WINDOW = 256
LENT = 1280
OWN = 640
EARLY = 12
MESH = pl.DeviceIdType.MESH


def kernel(nz, ny, pairs, elements, gaps_in, freqs_in, out, gaps, turned_gaps, weights, freqs,
           parts_a, parts_b, win, own_a, own_b, lent, got_win, got, wbuf, lhs,
           sum_own, sum_got, out_win, out_own, out_got, in_sem, part_sem, part_recv, part_send,
           nrecv, nsend, zrecv, zsend, xwrecv, xwsend, xrecv, xsend, wrecv, wsend, osem):
    row, col = lax.axis_index("row"), lax.axis_index("col")
    hi, z = row // nz, lax.rem(row, nz)
    ncol = ny * 4
    plane = 2 * ncol
    seat = hi * ncol + col
    y = col // 4
    in_y = lax.rem(col, 4)
    lo, core = in_y // 2, lax.rem(in_y, 2)
    up = (hi * nz + lax.rem(z + 1, nz), col)
    down = (hi * nz + lax.rem(z + nz - 1, nz), col)
    other_lo = y * 4 + (1 - lo) * 2 + core
    side = [(z, other_lo), (nz + z, other_lo)]
    in_column = [(row, lax.rem(y + k, ny) * 4 + in_y) for k in (1, 3, 2)]
    twin_core = (row, y * 4 + lo * 2 + (1 - core))
    half = nz // 2

    def seated(h, k):
        c = lax.rem(col + k, ncol)
        return h, c // 4, lax.rem(c, 4) // 2, lax.rem(c, 2)

    def device_at(h, y, lo, core):
        return h * nz + z, y * 4 + lo * 2 + core

    barrier = pltpu.get_barrier_semaphore()
    for device in (up, down):
        pl.semaphore_signal(barrier, inc=1, device_id=device, device_id_type=MESH)

    def for_others(do):
        pl.loop(1, ncol)(lambda k: do(seated(hi, k)))
        pl.loop(0, ncol)(lambda k: do(seated(1 - hi, k)))

    for_others(lambda to: pl.semaphore_signal(barrier, inc=1, device_id=device_at(*to), device_id_type=MESH))

    loads = [
        pltpu.make_async_copy(gaps_in, gaps, in_sem.at[0]),
        pltpu.make_async_copy(freqs_in, freqs, in_sem.at[1]),
    ]
    for load in loads:
        load.start()

    def lent_at(h, y):
        first = y // 2
        return pl.multiple_of((h + first - 2 * h * first) * LENT, 128)

    def lent_range(h, y, lo, core):
        return elements.at[y, 1 - lo, core, :, pl.ds(lent_at(h, y), LENT)]

    def own_range(h, y, lo, core):
        return elements.at[y, lo, core, :, pl.ds(2 * LENT, 2 * OWN)]

    ranges = ((lent_range, parts_a), (own_range, parts_b))
    mine = [
        pltpu.make_async_copy(source(hi, y, lo, core), parts.at[seat], part_sem.at[n])
        for n, (source, parts) in enumerate(ranges)
    ]
    for copy in mine:
        copy.start()
    pl.semaphore_wait(barrier, plane + 1)

    def remote(src, dst, send, recv, device):
        return pltpu.make_async_remote_copy(
            src_ref=src, dst_ref=dst, send_sem=send, recv_sem=recv, device_id=device, device_id_type=MESH
        )

    def wait(ref, sem):
        pltpu.make_async_copy(ref, ref, sem).wait()

    def exchange(n):
        source, parts = ranges[n]
        for_others(lambda to: remote(
            source(*to), parts.at[seat], part_send.at[n], part_recv.at[n, hi], device_at(*to)
        ).start())

    def exchanged(n, same):
        parts = ranges[n][1]
        if same:
            mine[n].wait()
        wait(parts.at[pl.ds(0, ncol - 1 if same else ncol)], part_recv.at[n, hi if same else 1 - hi])

    exchange(0)

    for load in loads:
        load.wait()
    for k in range(4):
        turned_gaps[k] = pltpu.roll(gaps[...], k * 32, 1)
    quarter = lax.broadcasted_iota(jnp.int32, (1, GSR), 1) // 32

    @pl.loop(0, pairs // GSR)
    def _(b):
        line = jnp.zeros((1, GSR), jnp.float32)
        for q in range(4):
            plane_at = lax.rem(z + (b if q < 2 else nz - 1 - b), nz)
            shift = lax.rem(q + 4 - lax.rem(plane_at, 4), 4)
            piece = turned_gaps[shift, pl.ds(q % 2 * 4 + plane_at // 4, 1), :]
            line = jnp.where(quarter == q, piece, line)
        for w in range(NW):
            weights[w, pl.ds(b, 1), :] = (
                -4.0 * line / ((line * line + freqs[w] * freqs[w]) * math.sqrt(pairs))
            )

    bufs = (lent, own_a, own_b)

    def begin(buf, h, parts, start):
        width = buf.shape[-1]
        part = parts[pl.ds(pl.multiple_of(h * ncol, ncol), ncol), :, start:start + width]
        buf[0, h] = part.reshape(2 * ncol, width)

    def place(way, s):
        return 0 if s == 0 else nz - 1 if s == half else 2 * s - 1 + way

    def push(first, count):
        late = int(first > EARLY)
        for n in range(2):
            remote(
                lent.at[pl.ds(first, count)], got.at[hi, pl.ds(first, count)],
                xsend.at[n], xrecv.at[hi, late], side[n],
            ).start()

    def arrived(n, h, way, s):
        wait(bufs[n].at[place(way, s), h], zrecv.at[way, n, h, s - 1])

    def tick(n, s, lanes=(0, 1)):
        for h in lanes:
            for way, device in ((0, up), (1, down)):
                if s > 0:
                    arrived(n, h, way, s)
                if s == half - 1 and way != h:
                    continue
                remote(
                    bufs[n].at[place(way, s), h], bufs[n].at[place(way, s + 1), h],
                    zsend.at[way, n, h], zrecv.at[way, n, h, s], device,
                ).start()

    def last(n):
        for h in range(2):
            arrived(n, h, h, half)

    def window_arrived(way, s):
        slab = win.at[place(way, s)]
        wait(slab.at[way] if s == half else slab, nrecv.at[way, s - 1])

    def window_tick(s):
        for way, device in ((0, up), (1, down)):
            if s > 0:
                window_arrived(way, s)
            src, dst = win.at[place(way, s)], win.at[place(way, s + 1)]
            if s == half - 1:
                src, dst = src.at[way], dst.at[way]
            remote(src, dst, nsend.at[way], nrecv.at[way, s], device).start()

    def window_push(first, count):
        for n in range(2):
            remote(
                win.at[pl.ds(first, count)], got_win.at[hi, pl.ds(first, count)],
                xwsend.at[n], xwrecv.at[hi], side[n],
            ).start()

    window_col = row // 2
    in_w = lax.rem(window_col, 4)
    same_core = core == lax.rem(in_w, 2)
    is_source = jnp.logical_and(same_core, y == window_col // 4)
    gathers = lo != in_w // 2

    def window_y():
        for h in range(2):
            wait(got_win.at[h], xwrecv.at[h])

        @pl.when(is_source)
        def _():
            for b in range(2):
                cut = slice(b * GSR, (b + 1) * GSR)
                this = lax.rem(row, 2) == b

                @pl.when(jnp.logical_and(this, gathers))
                def _():
                    wbuf[...] = win[:, :, :, cut]

                @pl.when(jnp.logical_and(this, jnp.logical_not(gathers)))
                def _():
                    wbuf[...] = got_win[hi, :, :, :, cut]
            for k, device in enumerate(in_column):
                remote(wbuf, wbuf, wsend.at[k], wrecv.at[0], device).start()

    def window_core():
        @pl.when(same_core)
        def _():
            @pl.when(jnp.logical_not(is_source))
            def _():
                wait(wbuf, wrecv.at[0])
            remote(wbuf, wbuf, wsend.at[ny - 1], wrecv.at[1], twin_core).start()

    def window_done():
        @pl.when(jnp.logical_not(same_core))
        def _():
            wait(wbuf, wrecv.at[1])

        @pl.loop(0, pairs // GSR)
        def _(b):
            at = pl.multiple_of(b * GSR, GSR)
            block = wbuf[pl.ds(b * 2, 2)].reshape(GSR, GSR)
            turned = block.astype(jnp.float32).T
            for w in range(NW):
                lhs[w * GSR:(w + 1) * GSR, pl.ds(at, GSR)] = (
                    turned * weights[w, pl.ds(b, 1), :]
                ).astype(jnp.bfloat16)

    early = EARLY * 4 * ncol

    def product(panel, low, high):
        return jnp.dot(
            lhs[:, low:high], panel.reshape(high - low, panel.shape[-1]), preferred_element_type=jnp.float32
        )

    def finish(chi, to, at, sem):
        to[...] = chi.astype(jnp.bfloat16).reshape(to.shape)
        write(to, at, sem).start()

    def write(to, at, sem):
        return pltpu.make_async_copy(to, out.at[:, :, pl.ds(at, to.shape[-1])], osem.at[sem])

    for same, h in ((True, hi), (False, 1 - hi)):
        exchanged(0, same)
        begin(lent, h, parts_a, WINDOW)
        tick(0, 0, (h,))
    for h in range(2):
        begin(win, h, parts_a, 0)
    window_tick(0)
    push(0, 1)
    exchange(1)
    window_tick(1)
    window_push(0, 3)
    for t in range(1, half + 1):
        if t < half // 2:
            window_tick(2 * t)
        if t == half // 2:
            for way in range(2):
                window_arrived(way, half)
            window_push(nz - 1, 1)
        if t == half // 2 + 1:
            window_y()
        if t < half:
            tick(0, t)
            push(place(0, t), 2)
        else:
            last(0)
            push(nz - 1, 1)
        if t < half // 2:
            window_tick(2 * t + 1)
            window_push(4 * t - 1, 4)
        if t == 1:
            for same, h in ((True, hi), (False, 1 - hi)):
                exchanged(1, same)
                for n in range(1, 3):
                    begin(bufs[n], h, parts_b, (n - 1) * OWN)
                    tick(n, 0, (h,))
        else:
            for n in range(1, 3):
                tick(n, t - 1)
        if t == half // 2 + 2:
            window_core()
        if t == half // 2 + 3:
            window_done()

            @pl.loop(0, 2)
            def _(h):
                finish(product(got_win[h], 0, pairs), out_win.at[h], lent_at(h, y), h)

    for n in range(2):
        sum_own[n] = product(bufs[1 + n][:EARLY], 0, early)

    @pl.loop(0, 2)
    def _(h):
        wait(got.at[h, pl.ds(0, EARLY + 1)], xrecv.at[h, 0])
        sum_got[h] = product(got[h, :EARLY], 0, early)

    for n in range(2):
        last(1 + n)
        finish(sum_own[n] + product(bufs[1 + n][EARLY:], early, pairs), out_own.at[n], 2 * LENT + n * OWN, 2 + n)

    @pl.loop(0, 2)
    def _(h):
        wait(got.at[h, pl.ds(EARLY + 1, nz - EARLY - 1)], xrecv.at[h, 1])
        finish(sum_got[h] + product(got[h, EARLY:], early, pairs), out_got.at[h], lent_at(h, y) + WINDOW, 4 + h)

    for way in range(2):
        wait(win.at[pl.ds(0, nz - 1), 0], nsend.at[way])
        for n in range(3):
            for h in range(2):
                wait(bufs[n].at[pl.ds(0, half if way == h else half - 1), h], zsend.at[way, n, h])
    for n in range(2):
        wait(lent, xsend.at[n])
        wait(win, xwsend.at[n])
    for n, parts in enumerate((parts_a, parts_b)):
        wait(parts.at[pl.ds(0, plane - 1)], part_send.at[n])

    @pl.when(is_source)
    def _():
        for k in range(ny - 1):
            wait(wbuf, wsend.at[k])

    @pl.when(same_core)
    def _():
        wait(wbuf, wsend.at[ny - 1])

    for h in range(2):
        write(out_own.at[h], 2 * LENT + h * OWN, 2 + h).wait()
        write(out_win.at[h], lent_at(h, y), h).wait()
        write(out_got.at[h], lent_at(h, y) + WINDOW, 4 + h).wait()


def on_device(pair_elements, energy_gaps, frequencies):
    rows, cols = lax.axis_size("row"), lax.axis_size("col")
    local, full = pair_elements.shape
    pairs = local * rows * cols
    block = full // cols
    nz, ny = rows // 2, cols // 4
    depth = local * cols
    plane = 2 * cols
    dma = pltpu.SemaphoreType.DMA

    def panels(width):
        return pltpu.VMEM((nz, 2, depth, width), jnp.bfloat16)

    operands = [
        pltpu.with_memory_space_constraint(operand, pltpu.HBM)
        for operand in (
            pair_elements.reshape(local, ny, 2, 2, block).transpose(1, 2, 3, 0, 4),
            energy_gaps.reshape(pairs // GSR, GSR),
            frequencies,
        )
    ]
    return pl.pallas_call(
        functools.partial(kernel, nz, ny, pairs),
        out_shape=jax.ShapeDtypeStruct((NW, GSR, block), jnp.bfloat16),
        in_specs=[pl.BlockSpec(memory_space=pl.ANY)] * 3,
        out_specs=pl.BlockSpec(memory_space=pl.ANY),
        scratch_shapes=[
            pltpu.VMEM((pairs // GSR, GSR), jnp.float32),
            pltpu.VMEM((4, pairs // GSR, GSR), jnp.float32),
            pltpu.VMEM((NW, pairs // GSR, GSR), jnp.float32),
            pltpu.SMEM((NW,), jnp.float32),
            pltpu.VMEM((plane, local, LENT), jnp.bfloat16),
            pltpu.VMEM((plane, local, 2 * OWN), jnp.bfloat16),
            panels(WINDOW),
            panels(OWN),
            panels(OWN),
            panels(LENT - WINDOW),
            pltpu.VMEM((2, nz, 2, depth, WINDOW), jnp.bfloat16),
            pltpu.VMEM((2, nz, 2, depth, LENT - WINDOW), jnp.bfloat16),
            panels(GSR),
            pltpu.VMEM((NW * GSR, pairs), jnp.bfloat16),
            pltpu.VMEM((2, NW * GSR, OWN), jnp.float32),
            pltpu.VMEM((2, NW * GSR, LENT - WINDOW), jnp.float32),
            pltpu.VMEM((2, NW, GSR, WINDOW), jnp.bfloat16),
            pltpu.VMEM((2, NW, GSR, OWN), jnp.bfloat16),
            pltpu.VMEM((2, NW, GSR, LENT - WINDOW), jnp.bfloat16),
            dma((2,)),
            dma((2,)),
            dma((2, 2)),
            dma((2,)),
            dma((2, nz // 2)),
            dma((2,)),
            dma((2, 3, 2, nz // 2)),
            dma((2, 3, 2)),
            dma((2,)),
            dma((2,)),
            dma((2, 2)),
            dma((2,)),
            dma((2,)),
            dma((ny,)),
            dma((6,)),
        ],
        compiler_params=pltpu.CompilerParams(
            collective_id=0, has_side_effects=True, vmem_limit_bytes=36 * 1024 * 1024
        ),
        cost_estimate=pl.CostEstimate(
            flops=2 * NW * GSR * pairs * block, bytes_accessed=2 * NW * GSR * block, transcendentals=0
        ),
    )(*operands)


def solution(mesh):
    in_specs = (P(("row", "col"), None), P(), P())
    out_specs = P(None, "row", "col")
    return jax.shard_map(
        on_device, mesh=mesh, in_specs=in_specs, out_specs=out_specs, check_vma=False
    )
```

profile of v0, /device:TPU:1, one launch (start us, length us, event | category | flops | bytes accessed | tf_op | source)
XLA Modules:
  0.0 83.4 jit_solution(675354396235616118)
XLA Ops:
  0.0 81.8 %shard_map.37 = bf16[3,128,3840]{2,1,0:T(8,128)(2,1)S(1)} custom-call(bf16[4,2,2,2,3840]{4,3,2,1,0:T(2,128)(2,1)} %bitcast.4, f32[8,128]{1,0:T(8,128)} %bitcast.5, f32[3]{0:T(128)} %freqs_in.1), custom_call_target="tpu_custom_call" | custom-call | flops 3019898880 | bytes 2949120 | tf_op jit(solution)/shard_map/pallas_call | solution.py:355
  81.8 1.6 %copy.5 = bf16[3,128,3840]{2,1,0:T(8,128)(2,1)} copy(bf16[3,128,3840]{2,1,0:T(8,128)(2,1)S(1)} %shard_map.37) | data formatting | bytes 5898240
where the time goes:
time: 84.6 us; the launch traced here: 83.4 us
  Pallas kernels  81.8 us (97%)
  local copies, waits for them, and re-layouts  1.6 us (2%)
    pallas_call x1, Pallas kernels, on_device(): pl.pallas_call(functools.partial(kernel, nz, ny, pairs), out_shape=jax.Sh...  81.8 us

commit v1 on v0

--- a/solution.py
+++ b/solution.py
@@ -101,25 +101,27 @@
         wait(parts.at[pl.ds(0, ncol - 1 if same else ncol)], part_recv.at[n, hi if same else 1 - hi])
 
     exchange(0)
-
-    for load in loads:
-        load.wait()
-    for k in range(4):
-        turned_gaps[k] = pltpu.roll(gaps[...], k * 32, 1)
-    quarter = lax.broadcasted_iota(jnp.int32, (1, GSR), 1) // 32
-
-    @pl.loop(0, pairs // GSR)
-    def _(b):
-        line = jnp.zeros((1, GSR), jnp.float32)
-        for q in range(4):
-            plane_at = lax.rem(z + (b if q < 2 else nz - 1 - b), nz)
-            shift = lax.rem(q + 4 - lax.rem(plane_at, 4), 4)
-            piece = turned_gaps[shift, pl.ds(q % 2 * 4 + plane_at // 4, 1), :]
-            line = jnp.where(quarter == q, piece, line)
-        for w in range(NW):
-            weights[w, pl.ds(b, 1), :] = (
-                -4.0 * line / ((line * line + freqs[w] * freqs[w]) * math.sqrt(pairs))
-            )
+    exchange(1)
+
+    def weigh():
+        for load in loads:
+            load.wait()
+        for k in range(4):
+            turned_gaps[k] = pltpu.roll(gaps[...], k * 32, 1)
+        quarter = lax.broadcasted_iota(jnp.int32, (1, GSR), 1) // 32
+
+        @pl.loop(0, pairs // GSR)
+        def _(b):
+            line = jnp.zeros((1, GSR), jnp.float32)
+            for q in range(4):
+                plane_at = lax.rem(z + (b if q < 2 else nz - 1 - b), nz)
+                shift = lax.rem(q + 4 - lax.rem(plane_at, 4), 4)
+                piece = turned_gaps[shift, pl.ds(q % 2 * 4 + plane_at // 4, 1), :]
+                line = jnp.where(quarter == q, piece, line)
+            for w in range(NW):
+                weights[w, pl.ds(b, 1), :] = (
+                    -4.0 * line / ((line * line + freqs[w] * freqs[w]) * math.sqrt(pairs))
+                )
 
     bufs = (lent, own_a, own_b)
 
@@ -249,7 +251,6 @@
         begin(win, h, parts_a, 0)
     window_tick(0)
     push(0, 1)
-    exchange(1)
     window_tick(1)
     window_push(0, 3)
     for t in range(1, half + 1):
@@ -279,6 +280,8 @@
         else:
             for n in range(1, 3):
                 tick(n, t - 1)
+        if t == 2:
+            weigh()
         if t == half // 2 + 2:
             window_core()
         if t == half // 2 + 3:
@@ -288,8 +291,9 @@
             def _(h):
                 finish(product(got_win[h], 0, pairs), out_win.at[h], lent_at(h, y), h)
 
-    for n in range(2):
-        sum_own[n] = product(bufs[1 + n][:EARLY], 0, early)
+            sum_own[0] = product(own_a[:EARLY], 0, early)
+
+    sum_own[1] = product(own_b[:EARLY], 0, early)
 
     @pl.loop(0, 2)
     def _(h):

time: 84.6 us -> 85.5 us (1.011)
  Pallas kernels: 81.8 us -> 83 us
    pallas_call x1, Pallas kernels: 81.8 us -> 83 us  [on_device(): pl.pallas_call(functools.partial(kernel, nz, ny, pairs), out_shape=jax.Sh...]
where the time goes in v1:
time: 85.5 us; the launch traced here: 84.6 us
  Pallas kernels  83 us (97%)
  local copies, waits for them, and re-layouts  1.6 us (2%)
    pallas_call x1, Pallas kernels, on_device(): pl.pallas_call(functools.partial(kernel, nz, ny, pairs), out_shape=jax.Sh...  83 us

profile of v1, /device:TPU:1, one launch (start us, length us, event | category | flops | bytes accessed | tf_op | source)
XLA Modules:
  0.0 84.6 jit_solution(8722719994030652777)
XLA Ops:
  0.0 83.0 %shard_map.37 = bf16[3,128,3840]{2,1,0:T(8,128)(2,1)S(1)} custom-call(bf16[4,2,2,2,3840]{4,3,2,1,0:T(2,128)(2,1)} %bitcast.4, f32[8,128]{1,0:T(8,128)} %bitcast.5, f32[3]{0:T(128)} %freqs_in.1), custom_call_target="tpu_custom_call" | custom-call | flops 3019898880 | bytes 2949120 | tf_op jit(solution)/shard_map/pallas_call | solution.py:359
  83.0 1.6 %copy.5 = bf16[3,128,3840]{2,1,0:T(8,128)(2,1)} copy(bf16[3,128,3840]{2,1,0:T(8,128)(2,1)S(1)} %shard_map.37) | data formatting | bytes 5898240

commit v2 on v1

--- a/solution.py
+++ b/solution.py
@@ -11,14 +11,16 @@
 NW = 3
 GSR = 128
 WINDOW = 256
-LENT = 1280
+LENT = 1024
 OWN = 640
+LENT_AT = 2 * WINDOW
+OWN_AT = LENT_AT + 2 * LENT
 EARLY = 12
 MESH = pl.DeviceIdType.MESH
 
 
 def kernel(nz, ny, pairs, elements, gaps_in, freqs_in, out, gaps, turned_gaps, weights, freqs,
-           parts_a, parts_b, win, own_a, own_b, lent, got_win, got, wbuf, lhs,
+           parts_lent, parts_win, parts_own, win, own_a, own_b, lent, got_win, got, wbuf, lhs,
            sum_own, sum_got, out_win, out_own, out_got, in_sem, part_sem, part_recv, part_send,
            nrecv, nsend, zrecv, zsend, xwrecv, xwsend, xrecv, xsend, wrecv, wsend, osem):
     row, col = lax.axis_index("row"), lax.axis_index("col")
@@ -48,8 +50,11 @@
     for device in (up, down):
         pl.semaphore_signal(barrier, inc=1, device_id=device, device_id_type=MESH)
 
+    def for_same(do):
+        pl.loop(1, ncol)(lambda k: do(seated(hi, k)))
+
     def for_others(do):
-        pl.loop(1, ncol)(lambda k: do(seated(hi, k)))
+        for_same(do)
         pl.loop(0, ncol)(lambda k: do(seated(1 - hi, k)))
 
     for_others(lambda to: pl.semaphore_signal(barrier, inc=1, device_id=device_at(*to), device_id_type=MESH))
@@ -61,19 +66,24 @@
     for load in loads:
         load.start()
 
-    def lent_at(h, y):
+    def window_at(h, y):
         first = y // 2
-        return pl.multiple_of((h + first - 2 * h * first) * LENT, 128)
+        return pl.multiple_of((h + first - 2 * h * first) * WINDOW, 128)
 
     def lent_range(h, y, lo, core):
-        return elements.at[y, 1 - lo, core, :, pl.ds(lent_at(h, y), LENT)]
+        return elements.at[y, 1 - lo, core, :, pl.ds(LENT_AT, 2 * LENT)]
+
+    def window_range(h, y, lo, core):
+        return elements.at[y, 1 - lo, core, :, pl.ds(window_at(h, y), WINDOW)]
 
     def own_range(h, y, lo, core):
-        return elements.at[y, lo, core, :, pl.ds(2 * LENT, 2 * OWN)]
-
-    ranges = ((lent_range, parts_a), (own_range, parts_b))
+        return elements.at[y, lo, core, :, pl.ds(OWN_AT, 2 * OWN)]
+
+    ranges = ((lent_range, parts_lent), (window_range, parts_win), (own_range, parts_own))
     mine = [
-        pltpu.make_async_copy(source(hi, y, lo, core), parts.at[seat], part_sem.at[n])
+        pltpu.make_async_copy(
+            source(hi, y, lo, core), parts.at[col if n == 0 else seat], part_sem.at[n]
+        )
         for n, (source, parts) in enumerate(ranges)
     ]
     for copy in mine:
@@ -90,8 +100,8 @@
 
     def exchange(n):
         source, parts = ranges[n]
-        for_others(lambda to: remote(
-            source(*to), parts.at[seat], part_send.at[n], part_recv.at[n, hi], device_at(*to)
+        (for_same if n == 0 else for_others)(lambda to: remote(
+            source(*to), parts.at[col if n == 0 else seat], part_send.at[n], part_recv.at[n, hi], device_at(*to)
         ).start())
 
     def exchanged(n, same):
@@ -100,8 +110,8 @@
             mine[n].wait()
         wait(parts.at[pl.ds(0, ncol - 1 if same else ncol)], part_recv.at[n, hi if same else 1 - hi])
 
-    exchange(0)
-    exchange(1)
+    for n in range(3):
+        exchange(n)
 
     def weigh():
         for load in loads:
@@ -123,7 +133,11 @@
                     -4.0 * line / ((line * line + freqs[w] * freqs[w]) * math.sqrt(pairs))
                 )
 
-    bufs = (lent, own_a, own_b)
+    owns = (own_a, own_b)
+
+    def slab(n, h, at):
+        return lent.at[h, at] if n == 0 else owns[n - 1].at[at, h]
+
 
     def begin(buf, h, parts, start):
         width = buf.shape[-1]
@@ -137,12 +151,12 @@
         late = int(first > EARLY)
         for n in range(2):
             remote(
-                lent.at[pl.ds(first, count)], got.at[hi, pl.ds(first, count)],
+                lent.at[:, pl.ds(first, count)], got.at[:, pl.ds(first, count), hi],
                 xsend.at[n], xrecv.at[hi, late], side[n],
             ).start()
 
     def arrived(n, h, way, s):
-        wait(bufs[n].at[place(way, s), h], zrecv.at[way, n, h, s - 1])
+        wait(slab(n, h, place(way, s)), zrecv.at[way, n, h, s - 1])
 
     def tick(n, s, lanes=(0, 1)):
         for h in lanes:
@@ -152,7 +166,7 @@
                 if s == half - 1 and way != h:
                     continue
                 remote(
-                    bufs[n].at[place(way, s), h], bufs[n].at[place(way, s + 1), h],
+                    slab(n, h, place(way, s)), slab(n, h, place(way, s + 1)),
                     zsend.at[way, n, h], zrecv.at[way, n, h, s], device,
                 ).start()
 
@@ -161,8 +175,8 @@
             arrived(n, h, h, half)
 
     def window_arrived(way, s):
-        slab = win.at[place(way, s)]
-        wait(slab.at[way] if s == half else slab, nrecv.at[way, s - 1])
+        part = win.at[place(way, s)]
+        wait(part.at[way] if s == half else part, nrecv.at[way, s - 1])
 
     def window_tick(s):
         for way, device in ((0, up), (1, down)):
@@ -243,14 +257,18 @@
     def write(to, at, sem):
         return pltpu.make_async_copy(to, out.at[:, :, pl.ds(at, to.shape[-1])], osem.at[sem])
 
+    def lent_at(j):
+        return pl.multiple_of(LENT_AT + j * LENT, 128)
+
+    exchanged(0, True)
+    for j in range(2):
+        lent[j, 0] = parts_lent[:, :, j * LENT:(j + 1) * LENT].reshape(2 * ncol, LENT)
+    tick(0, 0)
+    push(0, 1)
     for same, h in ((True, hi), (False, 1 - hi)):
-        exchanged(0, same)
-        begin(lent, h, parts_a, WINDOW)
-        tick(0, 0, (h,))
-    for h in range(2):
-        begin(win, h, parts_a, 0)
+        exchanged(1, same)
+        begin(win, h, parts_win, 0)
     window_tick(0)
-    push(0, 1)
     window_tick(1)
     window_push(0, 3)
     for t in range(1, half + 1):
@@ -273,9 +291,9 @@
             window_push(4 * t - 1, 4)
         if t == 1:
             for same, h in ((True, hi), (False, 1 - hi)):
-                exchanged(1, same)
+                exchanged(2, same)
                 for n in range(1, 3):
-                    begin(bufs[n], h, parts_b, (n - 1) * OWN)
+                    begin(owns[n - 1], h, parts_own, (n - 1) * OWN)
                     tick(n, 0, (h,))
         else:
             for n in range(1, 3):
@@ -289,36 +307,42 @@
 
             @pl.loop(0, 2)
             def _(h):
-                finish(product(got_win[h], 0, pairs), out_win.at[h], lent_at(h, y), h)
+                finish(product(got_win[h], 0, pairs), out_win.at[h], window_at(h, y), h)
 
             sum_own[0] = product(own_a[:EARLY], 0, early)
 
     sum_own[1] = product(own_b[:EARLY], 0, early)
 
+    for h in range(2):
+        wait(got.at[:, pl.ds(0, EARLY + 1), h], xrecv.at[h, 0])
+
     @pl.loop(0, 2)
-    def _(h):
-        wait(got.at[h, pl.ds(0, EARLY + 1)], xrecv.at[h, 0])
-        sum_got[h] = product(got[h, :EARLY], 0, early)
+    def _(j):
+        sum_got[j] = product(got[j, :EARLY], 0, early)
 
     for n in range(2):
         last(1 + n)
-        finish(sum_own[n] + product(bufs[1 + n][EARLY:], early, pairs), out_own.at[n], 2 * LENT + n * OWN, 2 + n)
+        finish(sum_own[n] + product(owns[n][EARLY:], early, pairs), out_own.at[n], OWN_AT + n * OWN, 2 + n)
+    for h in range(2):
+        wait(got.at[:, pl.ds(EARLY + 1, nz - EARLY - 1), h], xrecv.at[h, 1])
 
     @pl.loop(0, 2)
-    def _(h):
-        wait(got.at[h, pl.ds(EARLY + 1, nz - EARLY - 1)], xrecv.at[h, 1])
-        finish(sum_got[h] + product(got[h, EARLY:], early, pairs), out_got.at[h], lent_at(h, y) + WINDOW, 4 + h)
+    def _(j):
+        finish(sum_got[j] + product(got[j, EARLY:], early, pairs), out_got.at[j], lent_at(j), 4 + j)
 
     for way in range(2):
         wait(win.at[pl.ds(0, nz - 1), 0], nsend.at[way])
-        for n in range(3):
-            for h in range(2):
-                wait(bufs[n].at[pl.ds(0, half if way == h else half - 1), h], zsend.at[way, n, h])
+        for h in range(2):
+            count = half if way == h else half - 1
+            wait(lent.at[h, pl.ds(0, count)], zsend.at[way, 0, h])
+            for n in range(2):
+                wait(owns[n].at[pl.ds(0, count), h], zsend.at[way, 1 + n, h])
     for n in range(2):
         wait(lent, xsend.at[n])
         wait(win, xwsend.at[n])
-    for n, parts in enumerate((parts_a, parts_b)):
-        wait(parts.at[pl.ds(0, plane - 1)], part_send.at[n])
+    wait(parts_lent.at[pl.ds(0, ncol - 1)], part_send.at[0])
+    wait(parts_win.at[pl.ds(0, plane - 1)], part_send.at[1])
+    wait(parts_own.at[pl.ds(0, plane - 1)], part_send.at[2])
 
     @pl.when(is_source)
     def _():
@@ -330,9 +354,9 @@
         wait(wbuf, wsend.at[ny - 1])
 
     for h in range(2):
-        write(out_own.at[h], 2 * LENT + h * OWN, 2 + h).wait()
-        write(out_win.at[h], lent_at(h, y), h).wait()
-        write(out_got.at[h], lent_at(h, y) + WINDOW, 4 + h).wait()
+        write(out_own.at[h], OWN_AT + h * OWN, 2 + h).wait()
+        write(out_win.at[h], window_at(h, y), h).wait()
+        write(out_got.at[h], lent_at(h), 4 + h).wait()
 
 
 def on_device(pair_elements, energy_gaps, frequencies):
@@ -366,25 +390,26 @@
             pltpu.VMEM((4, pairs // GSR, GSR), jnp.float32),
             pltpu.VMEM((NW, pairs // GSR, GSR), jnp.float32),
             pltpu.SMEM((NW,), jnp.float32),
-            pltpu.VMEM((plane, local, LENT), jnp.bfloat16),
+            pltpu.VMEM((cols, local, 2 * LENT), jnp.bfloat16),
+            pltpu.VMEM((plane, local, WINDOW), jnp.bfloat16),
             pltpu.VMEM((plane, local, 2 * OWN), jnp.bfloat16),
             panels(WINDOW),
             panels(OWN),
             panels(OWN),
-            panels(LENT - WINDOW),
+            pltpu.VMEM((2, nz, depth, LENT), jnp.bfloat16),
             pltpu.VMEM((2, nz, 2, depth, WINDOW), jnp.bfloat16),
-            pltpu.VMEM((2, nz, 2, depth, LENT - WINDOW), jnp.bfloat16),
+            pltpu.VMEM((2, nz, 2, depth, LENT), jnp.bfloat16),
             panels(GSR),
             pltpu.VMEM((NW * GSR, pairs), jnp.bfloat16),
             pltpu.VMEM((2, NW * GSR, OWN), jnp.float32),
-            pltpu.VMEM((2, NW * GSR, LENT - WINDOW), jnp.float32),
+            pltpu.VMEM((2, NW * GSR, LENT), jnp.float32),
             pltpu.VMEM((2, NW, GSR, WINDOW), jnp.bfloat16),
             pltpu.VMEM((2, NW, GSR, OWN), jnp.bfloat16),
-            pltpu.VMEM((2, NW, GSR, LENT - WINDOW), jnp.bfloat16),
-            dma((2,)),
-            dma((2,)),
-            dma((2, 2)),
-            dma((2,)),
+            pltpu.VMEM((2, NW, GSR, LENT), jnp.bfloat16),
+            dma((2,)),
+            dma((3,)),
+            dma((3, 2)),
+            dma((3,)),
             dma((2, nz // 2)),
             dma((2,)),
             dma((2, 3, 2, nz // 2)),

time: 85.5 us -> 84.8 us (level)
  no operation moved by 1% of the time
where the time goes in v2:
time: 84.8 us; the launch traced here: 84.7 us
  Pallas kernels  83.1 us (98%)
  local copies, waits for them, and re-layouts  1.6 us (2%)
    pallas_call x1, Pallas kernels, on_device(): pl.pallas_call(functools.partial(kernel, nz, ny, pairs), out_shape=jax.Sh...  83.1 us

profile of v2, /device:TPU:1, one launch (start us, length us, event | category | flops | bytes accessed | tf_op | source)
XLA Modules:
  0.0 84.7 jit_solution(16307353068760205145)
XLA Ops:
  0.0 83.1 %shard_map.37 = bf16[3,128,3840]{2,1,0:T(8,128)(2,1)S(1)} custom-call(bf16[4,2,2,2,3840]{4,3,2,1,0:T(2,128)(2,1)} %bitcast.4, f32[8,128]{1,0:T(8,128)} %bitcast.5, f32[3]{0:T(128)} %freqs_in.1), custom_call_target="tpu_custom_call" | custom-call | flops 3019898880 | bytes 2949120 | tf_op jit(solution)/shard_map/pallas_call | solution.py:383
  83.1 1.6 %copy.5 = bf16[3,128,3840]{2,1,0:T(8,128)(2,1)} copy(bf16[3,128,3840]{2,1,0:T(8,128)(2,1)S(1)} %shard_map.37) | data formatting | bytes 5898240

commit v3 on v2

--- a/solution.py
+++ b/solution.py
@@ -110,7 +110,7 @@
             mine[n].wait()
         wait(parts.at[pl.ds(0, ncol - 1 if same else ncol)], part_recv.at[n, hi if same else 1 - hi])
 
-    for n in range(3):
+    for n in range(2):
         exchange(n)
 
     def weigh():
@@ -265,6 +265,7 @@
         lent[j, 0] = parts_lent[:, :, j * LENT:(j + 1) * LENT].reshape(2 * ncol, LENT)
     tick(0, 0)
     push(0, 1)
+    exchange(2)
     for same, h in ((True, hi), (False, 1 - hi)):
         exchanged(1, same)
         begin(win, h, parts_win, 0)
@@ -320,15 +321,16 @@
     def _(j):
         sum_got[j] = product(got[j, :EARLY], 0, early)
 
+    for h in range(2):
+        wait(got.at[:, pl.ds(EARLY + 1, nz - EARLY - 1), h], xrecv.at[h, 1])
+
+    @pl.loop(0, 2)
+    def _(j):
+        finish(sum_got[j] + product(got[j, EARLY:], early, pairs), out_got.at[j], lent_at(j), 4 + j)
+
     for n in range(2):
         last(1 + n)
         finish(sum_own[n] + product(owns[n][EARLY:], early, pairs), out_own.at[n], OWN_AT + n * OWN, 2 + n)
-    for h in range(2):
-        wait(got.at[:, pl.ds(EARLY + 1, nz - EARLY - 1), h], xrecv.at[h, 1])
-
-    @pl.loop(0, 2)
-    def _(j):
-        finish(sum_got[j] + product(got[j, EARLY:], early, pairs), out_got.at[j], lent_at(j), 4 + j)
 
     for way in range(2):
         wait(win.at[pl.ds(0, nz - 1), 0], nsend.at[way])

time: 84.8 us -> 84.6 us (level)
  no operation moved by 1% of the time
where the time goes in v3:
time: 84.6 us; the launch traced here: 84.5 us
  Pallas kernels  82.8 us (98%)
  local copies, waits for them, and re-layouts  1.6 us (2%)
    pallas_call x1, Pallas kernels, on_device(): pl.pallas_call(functools.partial(kernel, nz, ny, pairs), out_shape=jax.Sh...  82.8 us

profile of v3, /device:TPU:1, one launch (start us, length us, event | category | flops | bytes accessed | tf_op | source)
XLA Modules:
  0.0 84.5 jit_solution(11189648096369557501)
XLA Ops:
  0.0 82.8 %shard_map.37 = bf16[3,128,3840]{2,1,0:T(8,128)(2,1)S(1)} custom-call(bf16[4,2,2,2,3840]{4,3,2,1,0:T(2,128)(2,1)} %bitcast.4, f32[8,128]{1,0:T(8,128)} %bitcast.5, f32[3]{0:T(128)} %freqs_in.1), custom_call_target="tpu_custom_call" | custom-call | flops 3019898880 | bytes 2949120 | tf_op jit(solution)/shard_map/pallas_call | solution.py:385
  82.8 1.6 %copy.5 = bf16[3,128,3840]{2,1,0:T(8,128)(2,1)} copy(bf16[3,128,3840]{2,1,0:T(8,128)(2,1)S(1)} %shard_map.37) | data formatting | bytes 5898240

commit v4 on v3

--- a/solution.py
+++ b/solution.py
@@ -147,11 +147,11 @@
     def place(way, s):
         return 0 if s == 0 else nz - 1 if s == half else 2 * s - 1 + way
 
-    def push(first, count):
+    def push(j, first, count):
         late = int(first > EARLY)
         for n in range(2):
             remote(
-                lent.at[:, pl.ds(first, count)], got.at[:, pl.ds(first, count), hi],
+                lent.at[j, pl.ds(first, count)], got.at[j, pl.ds(first, count), hi],
                 xsend.at[n], xrecv.at[hi, late], side[n],
             ).start()
 
@@ -264,7 +264,8 @@
     for j in range(2):
         lent[j, 0] = parts_lent[:, :, j * LENT:(j + 1) * LENT].reshape(2 * ncol, LENT)
     tick(0, 0)
-    push(0, 1)
+    for j in range(2):
+        push(j, 0, 1)
     exchange(2)
     for same, h in ((True, hi), (False, 1 - hi)):
         exchanged(1, same)
@@ -283,10 +284,11 @@
             window_y()
         if t < half:
             tick(0, t)
-            push(place(0, t), 2)
+            push(0, place(0, t), 2)
         else:
             last(0)
-            push(nz - 1, 1)
+            for j in range(2):
+                push(j, nz - 1, 1)
         if t < half // 2:
             window_tick(2 * t + 1)
             window_push(4 * t - 1, 4)
@@ -296,9 +298,12 @@
                 for n in range(1, 3):
                     begin(owns[n - 1], h, parts_own, (n - 1) * OWN)
                     tick(n, 0, (h,))
+            push(1, 1, 2)
         else:
-            for n in range(1, 3):
-                tick(n, t - 1)
+            tick(1, t - 1)
+            if t < half:
+                push(1, place(0, t), 2)
+            tick(2, t - 1)
         if t == 2:
             weigh()
         if t == half // 2 + 2:

time: 84.6 us -> 85 us (level)
  no operation moved by 1% of the time
where the time goes in v4:
time: 85 us; the launch traced here: 84.7 us
  Pallas kernels  83.1 us (98%)
  local copies, waits for them, and re-layouts  1.6 us (2%)
    pallas_call x1, Pallas kernels, on_device(): pl.pallas_call(functools.partial(kernel, nz, ny, pairs), out_shape=jax.Sh...  83.1 us

profile of v4, /device:TPU:1, one launch (start us, length us, event | category | flops | bytes accessed | tf_op | source)
XLA Modules:
  0.0 84.7 jit_solution(12839036738502023780)
XLA Ops:
  0.0 83.1 %shard_map.37 = bf16[3,128,3840]{2,1,0:T(8,128)(2,1)S(1)} custom-call(bf16[4,2,2,2,3840]{4,3,2,1,0:T(2,128)(2,1)} %bitcast.4, f32[8,128]{1,0:T(8,128)} %bitcast.5, f32[3]{0:T(128)} %freqs_in.1), custom_call_target="tpu_custom_call" | custom-call | flops 3019898880 | bytes 2949120 | tf_op jit(solution)/shard_map/pallas_call | solution.py:390
  83.1 1.6 %copy.5 = bf16[3,128,3840]{2,1,0:T(8,128)(2,1)} copy(bf16[3,128,3840]{2,1,0:T(8,128)(2,1)S(1)} %shard_map.37) | data formatting | bytes 5898240

commit v5 on v3

--- a/solution.py
+++ b/solution.py
@@ -11,8 +11,8 @@
 NW = 3
 GSR = 128
 WINDOW = 256
-LENT = 1024
-OWN = 640
+LENT = 896
+OWN = 768
 LENT_AT = 2 * WINDOW
 OWN_AT = LENT_AT + 2 * LENT
 EARLY = 12

time: 84.6 us -> 86.5 us (1.022)
  Pallas kernels: 82.8 us -> 84 us
    pallas_call x1, Pallas kernels: 82.8 us -> 84 us  [on_device(): pl.pallas_call(functools.partial(kernel, nz, ny, pairs), out_shape=jax.Sh...]
where the time goes in v5:
time: 86.5 us; the launch traced here: 85.6 us
  Pallas kernels  84 us (97%)
  local copies, waits for them, and re-layouts  1.6 us (2%)
    pallas_call x1, Pallas kernels, on_device(): pl.pallas_call(functools.partial(kernel, nz, ny, pairs), out_shape=jax.Sh...  84 us

profile of v5, /device:TPU:1, one launch (start us, length us, event | category | flops | bytes accessed | tf_op | source)
XLA Modules:
  0.0 85.6 jit_solution(12221015206470366330)
XLA Ops:
  0.0 84.0 %shard_map.37 = bf16[3,128,3840]{2,1,0:T(8,128)(2,1)S(1)} custom-call(bf16[4,2,2,2,3840]{4,3,2,1,0:T(2,128)(2,1)} %bitcast.4, f32[8,128]{1,0:T(8,128)} %bitcast.5, f32[3]{0:T(128)} %freqs_in.1), custom_call_target="tpu_custom_call" | custom-call | flops 3019898880 | bytes 2949120 | tf_op jit(solution)/shard_map/pallas_call | solution.py:385
  84.0 1.6 %copy.5 = bf16[3,128,3840]{2,1,0:T(8,128)(2,1)} copy(bf16[3,128,3840]{2,1,0:T(8,128)(2,1)S(1)} %shard_map.37) | data formatting | bytes 5898240

commit v6 on v3

--- a/solution.py
+++ b/solution.py
@@ -284,9 +284,6 @@
         if t < half:
             tick(0, t)
             push(place(0, t), 2)
-        else:
-            last(0)
-            push(nz - 1, 1)
         if t < half // 2:
             window_tick(2 * t + 1)
             window_push(4 * t - 1, 4)
@@ -304,6 +301,8 @@
         if t == half // 2 + 2:
             window_core()
         if t == half // 2 + 3:
+            last(0)
+            push(nz - 1, 1)
             window_done()
 
             @pl.loop(0, 2)

time: 84.6 us -> 84.6 us (level)
  no operation moved by 1% of the time
where the time goes in v6:
time: 84.6 us; the launch traced here: 84.5 us
  Pallas kernels  82.8 us (98%)
  local copies, waits for them, and re-layouts  1.6 us (2%)
    pallas_call x1, Pallas kernels, on_device(): pl.pallas_call(functools.partial(kernel, nz, ny, pairs), out_shape=jax.Sh...  82.8 us

profile of v6, /device:TPU:1, one launch (start us, length us, event | category | flops | bytes accessed | tf_op | source)
XLA Modules:
  0.0 84.5 jit_solution(15615063442640101827)
XLA Ops:
  0.0 82.8 %shard_map.37 = bf16[3,128,3840]{2,1,0:T(8,128)(2,1)S(1)} custom-call(bf16[4,2,2,2,3840]{4,3,2,1,0:T(2,128)(2,1)} %bitcast.4, f32[8,128]{1,0:T(8,128)} %bitcast.5, f32[3]{0:T(128)} %freqs_in.1), custom_call_target="tpu_custom_call" | custom-call | flops 3019898880 | bytes 2949120 | tf_op jit(solution)/shard_map/pallas_call | solution.py:384
  82.8 1.6 %copy.5 = bf16[3,128,3840]{2,1,0:T(8,128)(2,1)} copy(bf16[3,128,3840]{2,1,0:T(8,128)(2,1)S(1)} %shard_map.37) | data formatting | bytes 5898240
